TPU v7x, 32 devices: a whole 2x2x4 slice. The times are simulated.
32 devices in a mesh: batch: 4 (over x, core), ctx: 8 (over z, y).
Axes of the slice: x: 2, y: 2, z: 4, core: 2. Of those that a mesh axis runs over, the one named last changes fastest.
Arguments:
- lengths: int32 [64], P('batch'), parts along dimension 0, may hold values from 1 to 2560, 4096 in all
- queries: bfloat16 [16384, 512], P(('batch', 'ctx')), parts along dimension 0, may hold values from -256 to 256
- key_rows: bfloat16 [16384, 128], P(('batch', 'ctx')), parts along dimension 0, may hold values from -4.5 to 4.5
- values: bfloat16 [16384, 128], P(('batch', 'ctx')), parts along dimension 0, may hold values from -6 to 6
Outputs:
- attended: bfloat16 [16384, 512], P(('batch', 'ctx')), parts along dimension 0
- log_mass: float32 [4, 16384], P(None, ('batch', 'ctx')), parts along dimension 1
There are 4 independent parts, one for each index of `batch`. A program takes and returns all parts, laid end to end along the dimension named above; each array names one. Nothing has to cross between parts.
Inputs may be any that keep to these rules, and one draw needn't show every extreme that they name: The lengths sum to 4096; the longest is exactly 2560.
All inputs are finite; a program needn't handle non-finite values.
Results may differ from a plain program's by a relative error of at most 0.0035.
Values may be sent and summed in bfloat16 or wider, within the bound.
No kernel may reach another device: no remote copies, remote signals or barrier semaphores. Data moves between devices by JAX's collectives and lax.ppermute only.
A program may use at most 64 MiB of HBM per device.

v0:
```python
import functools
import math

import jax
import jax.numpy as jnp
from jax import lax
from jax.experimental import pallas as pl
from jax.experimental.pallas import tpu as pltpu
from jax.sharding import PartitionSpec as P

QH = 4
HD = 128
LOW = -1e30
SCALE = 1.0 / math.sqrt(HD)
EXP2_SCALE = SCALE * math.log2(math.e)
VMEM_LIMIT = 32 * 1024 * 1024
LITTLE = pl.CostEstimate(flops=1024, bytes_accessed=1024, transcendentals=0)


def dot(a, b):
    return jnp.dot(a, b, preferred_element_type=jnp.float32)


def own_kernel(lengths_ref, q_ref, kv_ref, qt_ref, acc_ref, stat_ref):
    q_rows = q_ref.shape[0]
    tile = math.gcd(q_rows, 128)
    own_first = lax.axis_index("ctx") * q_rows
    ends = []
    end = jnp.int32(0)
    for d in range(lengths_ref.shape[0]):
        end = end + lengths_ref[d]
        ends.append(end - own_first)
    values_t = jnp.transpose(kv_ref[q_rows:])
    for h in range(QH):
        qt_ref[h] = jnp.transpose(q_ref[:, h * HD : (h + 1) * HD])
    for t in range(q_rows // tile):
        keys = (t + 1) * tile
        here = slice(t * tile, (t + 1) * tile)
        row = lax.broadcasted_iota(jnp.int32, (1, tile), 1) + t * tile
        start = jnp.zeros((1, tile), jnp.int32)
        for end in ends:
            start = jnp.where(row >= end, jnp.maximum(start, end), start)
        key = lax.broadcasted_iota(jnp.int32, (keys, tile), 0)
        hidden = (key < start) | (key > row)
        hidden = jnp.concatenate([hidden] * QH, axis=1)
        heads = jnp.concatenate([qt_ref[h, :, here] for h in range(QH)], axis=1)
        scores = jnp.where(hidden, LOW, dot(kv_ref[:keys, :], heads))
        top = jnp.max(scores, axis=0, keepdims=True)
        weights = jnp.exp2((scores - top) * EXP2_SCALE)
        total = jnp.sum(weights, axis=0, keepdims=True)
        mixed = dot(values_t[:, :keys], weights.astype(jnp.bfloat16))
        for h in range(QH):
            part = slice(h * tile, (h + 1) * tile)
            acc_ref[h, :, here] = mixed[:, part]
            stat_ref[h : h + 1, here] = top[:, part]
            stat_ref[QH + h : QH + h + 1, here] = total[:, part]


def past_kernel(distances, is_last, lengths_ref, qt_ref, acc_in, stat_in, *refs):
    kv_refs = refs[: len(distances)]
    acc_ref, stat_ref = refs[len(distances) : len(distances) + 2]
    q_rows = qt_ref.shape[2]
    half = q_rows // 2
    here = lax.axis_index("ctx")
    odd = here % 2
    own_first = here * q_rows
    first = own_first
    last = own_first
    end = jnp.int32(0)
    for d in range(lengths_ref.shape[0]):
        begin, end = end, end + lengths_ref[d]
        holds = (begin < own_first) & (end > own_first)
        first = jnp.where(holds, begin, first)
        last = jnp.where(holds, end, last)
    live_rows = last - own_first

    def side_by_side(read):
        return jnp.concatenate([read(h) for h in range(QH)], axis=1)

    def absorb(kv_ref, rows, cols, skipped=0, cut=None):
        live = lax.broadcasted_iota(jnp.int32, (1, rows), 1) + cols.start < live_rows
        live = side_by_side(lambda h: live)
        scores = dot(kv_ref[skipped:q_rows], side_by_side(lambda h: qt_ref[h, :, cols]))
        if cut is not None:
            hidden = lax.broadcasted_iota(jnp.int32, scores.shape, 0) + skipped < cut
            scores = jnp.where(hidden, LOW, scores)
        old_top = side_by_side(lambda h: stat_ref[h : h + 1, cols])
        old_total = side_by_side(lambda h: stat_ref[QH + h : QH + h + 1, cols])
        top = jnp.maximum(old_top, jnp.max(scores, axis=0, keepdims=True))
        top = jnp.where(live, top, old_top)
        weights = jnp.exp2((scores - top) * EXP2_SCALE)
        total = jnp.sum(weights, axis=0, keepdims=True)
        mixed = dot(jnp.transpose(kv_ref[q_rows + skipped :]), weights.astype(jnp.bfloat16))
        decay = jnp.exp2((old_top - top) * EXP2_SCALE)
        total = old_total * decay + jnp.where(live, total, 0.0)
        mixed = jnp.where(live, mixed, 0.0)
        for h in range(QH):
            part = slice(h * rows, (h + 1) * rows)
            acc_ref[h, :, cols] = acc_ref[h, :, cols] * decay[:, part] + mixed[:, part]
            stat_ref[h : h + 1, cols] = top[:, part]
            stat_ref[QH + h : QH + h + 1, cols] = total[:, part]

    def absorb_tiles(kv_ref, skipped, cut):
        def absorb_tile(t, _):
            cols = pl.ds(pl.multiple_of(t * half, half), half)
            absorb(kv_ref, half, cols, skipped, cut)
            return 0

        lax.fori_loop(0, jnp.where(live_rows > half, 2, 1), absorb_tile, 0)

    last_pair = here >= lax.axis_size("ctx") - 2
    for kv_ref, (even_distance, odd_distance, only) in zip(kv_refs, distances):
        distance = jnp.where(odd == 1, odd_distance, even_distance)
        cut = first - (here - distance) * q_rows
        seen = (distance > 0) & (live_rows > 0) & (cut < q_rows)
        if only is not None:
            seen = seen & (last_pair == only)
        wide = (cut <= 0) & (live_rows > half)
        pl.when(seen & wide)(functools.partial(absorb, kv_ref, q_rows, slice(0, q_rows)))
        pl.when(seen & jnp.logical_not(wide) & (cut < half))(
            functools.partial(absorb_tiles, kv_ref, 0, cut)
        )
        pl.when(seen & (cut >= half))(functools.partial(absorb_tiles, kv_ref, half, cut))

    if is_last:
        out_ref, mass_ref = refs[len(distances) + 2 :]
        for h in range(QH):
            mixed = acc_ref[h] * (1.0 / stat_ref[QH + h : QH + h + 1, :])
            out_ref[:, h * HD : (h + 1) * HD] = jnp.transpose(mixed.astype(jnp.bfloat16))
        mass_ref[...] = stat_ref[:QH, :] * SCALE + jnp.log(stat_ref[QH:, :])


def state_shapes(q_rows):
    return (
        jax.ShapeDtypeStruct((QH, HD, q_rows), jnp.float32),
        jax.ShapeDtypeStruct((2 * QH, q_rows), jnp.float32),
    )


def own_part(lengths, queries, own):
    q_rows = queries.shape[0]
    in_smem = pl.BlockSpec(memory_space=pltpu.SMEM)
    in_vmem = pl.BlockSpec(memory_space=pltpu.VMEM)
    qt, *state = pl.pallas_call(
        own_kernel,
        out_shape=(jax.ShapeDtypeStruct((QH, HD, q_rows), jnp.bfloat16),) + state_shapes(q_rows),
        in_specs=[in_smem, in_vmem, in_vmem],
        out_specs=(in_vmem, in_vmem, in_vmem),
        compiler_params=pltpu.CompilerParams(vmem_limit_bytes=VMEM_LIMIT),
        cost_estimate=LITTLE,
    )(lengths, queries, own)
    return qt, state


def past_part(lengths, qt, state, shards, is_last=False):
    q_rows = qt.shape[2]
    distances = [s[0] for s in shards]
    arrays = [s[1] for s in shards]
    in_smem = pl.BlockSpec(memory_space=pltpu.SMEM)
    in_vmem = pl.BlockSpec(memory_space=pltpu.VMEM)
    out_shape = state_shapes(q_rows)
    if is_last:
        out_shape += (
            jax.ShapeDtypeStruct((q_rows, QH * HD), jnp.bfloat16),
            jax.ShapeDtypeStruct((QH, q_rows), jnp.float32),
        )
    outs = pl.pallas_call(
        functools.partial(past_kernel, distances, is_last),
        out_shape=out_shape,
        in_specs=[in_smem] + [in_vmem] * (3 + len(arrays)),
        out_specs=(in_vmem,) * len(out_shape),
        input_output_aliases={2: 0, 3: 1},
        compiler_params=pltpu.CompilerParams(vmem_limit_bytes=VMEM_LIMIT),
        cost_estimate=LITTLE,
    )(lengths, qt, *state, *arrays)
    return outs[2:] if is_last else outs


def on_device(lengths, queries, key_rows, values):
    count = lax.axis_size("ctx")
    reach = min(count // 2 + 1, count - 1)
    strides = reach // 2

    def send(value, pairs):
        return lax.ppermute(value, "ctx", pairs)

    own = jnp.concatenate([key_rows, values])
    moving = send(own, [(i, i + 2) for i in range(count - 2)])
    qt, state = own_part(lengths, queries, own)
    own, *state = lax.optimization_barrier((own, *state))
    pairs = [(i, i + 1) for i in range(0, count, 2)]
    if reach % 2 == 1:
        pairs += [(i + 1, i) for i in range(0, count - reach - 1, 2)]
    beside = first_beside = send(own, pairs)
    moving, *state = lax.optimization_barrier((moving, *state))
    early, side = [((0, 1, True), beside)], [((0, 1, False), beside)]
    for k in range(1, strides + 1):
        arrived = moving
        if k < strides:
            moving = send(arrived, [(i, i + 2) for i in range(2 * k, count - 2)])
        exchange = [(i + 1, i) for i in range(2 * k, count, 2)]
        distances = (2 * k - 1, 0, None)
        if 2 * k + 1 <= reach:
            exchange += [(i, i + 1) for i in range(2 * k, count, 2)]
            distances = (2 * k - 1, 2 * k + 1, None)
        shards = [((2 * k, 2 * k, None), arrived)] + (early if k == 1 else side)
        side = (side if k == 1 else []) + [(distances, send(arrived, exchange))]
        state = past_part(lengths, qt, state, shards)
        if k == strides - 1 and reach % 2 == 1:
            first_beside, *state = lax.optimization_barrier((first_beside, *state))
            far = send(first_beside, [(i, i + reach + 1) for i in range(0, count - reach - 1, 2)])
        if k < strides:
            moving, *state = lax.optimization_barrier((moving, *state))
    if reach % 2 == 1:
        side.insert(0, ((reach, 0, None), far))
    return past_part(lengths, qt, state, side, is_last=True)


def solution(mesh):
    in_specs = (
        P("batch"),
        P(("batch", "ctx"), None),
        P(("batch", "ctx"), None),
        P(("batch", "ctx"), None),
    )
    out_specs = (P(("batch", "ctx"), None), P(None, ("batch", "ctx")))
    return jax.shard_map(
        on_device, mesh=mesh, in_specs=in_specs, out_specs=out_specs, check_vma=False
    )
```

profile of v0, /device:TPU:16, one launch (start us, length us, event | category | flops | bytes accessed | tf_op | source)
XLA Modules:
  0.0 34.3 jit_solution(12347392588503718197)
XLA Ops:
  0.6 0.0 copy-start.2
  0.6 0.9 %constant_dynamic-update-slice_fusion.1 = bf16[1024,128]{1,0:T(8,128)(2,1)S(1)} fusion(bf16[512,128]{1,0:T(8,128)(2,1)} %param.6), kind=kLoop, calls=%fused_computation.1 | loop fusion | bytes 262144
  1.6 0.0 copy-done.2
  1.6 0.0 copy-start.1
  1.6 3.5 %collective-permute-start = (bf16[1024,128]{1,0:T(8,128)(2,1)S(1)}, bf16[1024,128]{1,0:T(8,128)(2,1)S(1)}, u32[]{:S(2)}, u32[]{:S(2)}) collective-permute-start(bf16[1024,128]{1,0:T(8,128)(2,1)S(1)} %constant_dynamic-update-slice_fusion.kv_ref), channel_id=1, source_target_pairs={{0,2},{1,3},{2,4},{3,5},{4,6},{5,7},{8,10},{9,11},{10,12},{11,13},... | collective-permute-start | bytes 786440 | tf_op jit(solution)/shard_map/ppermute | solution.py:185
  5.1 0.0 copy-done.1
  5.1 0.0 copy-start
  5.2 1.0 %copy-done = bf16[512,512]{1,0:T(8,128)(2,1)S(1)} copy-done((bf16[512,512]{1,0:T(8,128)(2,1)S(1)}, bf16[512,512]{1,0:T(8,128)(2,1)}, u32[]{:S(2)}) %copy-start) | copy-done | bytes 524312
  6.2 2.3 %shard_map.59 = (bf16[4,128,512]{2,1,0:T(8,128)(2,1)S(1)}, f32[4,128,512]{2,1,0:T(8,128)S(1)}, f32[8,512]{1,0:T(8,128)S(1)}) custom-call(s32[16]{0:T(128)S(1)} %copy-done.1, bf16[512,512]{1,0:T(8,128)(2,1)S(1)} %copy-done, bf16[1024,128]{1,0:T(8,128)(2,1)S(1)} %constant_dynamic-update-slice_fusion.kv_ref), custom_call_target="tpu_custom_call" | custom-call | flops 1024 | bytes 1024 | tf_op jit(solution)/shard_map/pallas_call | solution.py:144
  8.5 3.4 %collective-permute-start.2 = (bf16[1024,128]{1,0:T(8,128)(2,1)S(1)}, bf16[1024,128]{1,0:T(8,128)(2,1)S(1)}, u32[]{:S(2)}, u32[]{:S(2)}) collective-permute-start(bf16[1024,128]{1,0:T(8,128)(2,1)S(1)} %constant_dynamic-update-slice_fusion.kv_ref), channel_id=1, source_target_pairs={{0,1},{2,3},{4,5},{6,7},{1,0},{8,9},{10,11},{12,13},{14,15},{9,8},... | collective-permute-start | bytes 786440 | tf_op jit(solution)/shard_map/ppermute | solution.py:185
  12.0 0.0 collective-permute-done.refs_0_
  12.0 3.1 %collective-permute-start.1 = (bf16[1024,128]{1,0:T(8,128)(2,1)S(1)}, bf16[1024,128]{1,0:T(8,128)(2,1)S(1)}, u32[]{:S(2)}, u32[]{:S(2)}) collective-permute-start(bf16[1024,128]{1,0:T(8,128)(2,1)S(1)} %collective-permute-done.refs_0_), channel_id=1, source_target_pairs={{2,4},{3,5},{4,6},{5,7},{10,12},{11,13},{12,14},{13,15},{18,20},{1... | collective-permute-start | bytes 786440 | tf_op jit(solution)/shard_map/ppermute | solution.py:185
  15.1 3.4 %collective-permute-start.3 = (bf16[1024,128]{1,0:T(8,128)(2,1)S(1)}, bf16[1024,128]{1,0:T(8,128)(2,1)S(1)}, u32[]{:S(2)}, u32[]{:S(2)}) collective-permute-start(bf16[1024,128]{1,0:T(8,128)(2,1)S(1)} %collective-permute-done.refs_0_), channel_id=1, source_target_pairs={{3,2},{5,4},{7,6},{2,3},{4,5},{6,7},{11,10},{13,12},{15,14},{10,11... | collective-permute-start | bytes 786440 | tf_op jit(solution)/shard_map/ppermute | solution.py:185
  18.5 0.0 collective-permute-done.2.refs_1_
  18.5 2.3 %shard_map.60 = (f32[4,128,512]{2,1,0:T(8,128)S(1)}, f32[8,512]{1,0:T(8,128)S(1)}) custom-call(s32[16]{0:T(128)S(1)} %copy-done.1, bf16[4,128,512]{2,1,0:T(8,128)(2,1)S(1)} %get-tuple-element.23.qt_ref, f32[4,128,512]{2,1,0:T(8,128)S(1)} %get-tuple-element.30.acc_in, ...), custom_call_target="tpu_custom_call", output_to_operand_aliasing={{0}: (2, {}), {1}: (3, {})} | custom-call | flops 1024 | bytes 1024 | tf_op jit(solution)/shard_map/pallas_call | solution.py:167
  20.8 0.7 %collective-permute-start.4 = (bf16[1024,128]{1,0:T(8,128)(2,1)S(1)}, bf16[1024,128]{1,0:T(8,128)(2,1)S(1)}, u32[]{:S(2)}, u32[]{:S(2)}) collective-permute-start(bf16[1024,128]{1,0:T(8,128)(2,1)S(1)} %collective-permute-done.2.refs_1_), channel_id=1, source_target_pairs={{0,6},{8,14},{16,22},{24,30}} | collective-permute-start | bytes 786440 | tf_op jit(solution)/shard_map/ppermute | solution.py:185
  21.5 0.0 collective-permute-done.1.refs_0_
  21.5 3.1 %collective-permute-start.5 = (bf16[1024,128]{1,0:T(8,128)(2,1)S(1)}, bf16[1024,128]{1,0:T(8,128)(2,1)S(1)}, u32[]{:S(2)}, u32[]{:S(2)}) collective-permute-start(bf16[1024,128]{1,0:T(8,128)(2,1)S(1)} %collective-permute-done.1.refs_0_), channel_id=1, source_target_pairs={{5,4},{7,6},{4,5},{6,7},{13,12},{15,14},{12,13},{14,15},{21,20},{2... | collective-permute-start | bytes 786440 | tf_op jit(solution)/shard_map/ppermute | solution.py:185
  24.6 0.0 collective-permute-done.3.refs_2_
  24.6 2.5 %shard_map.61 = (f32[4,128,512]{2,1,0:T(8,128)S(1)}, f32[8,512]{1,0:T(8,128)S(1)}) custom-call(s32[16]{0:T(128)S(1)} %copy-done.1, bf16[4,128,512]{2,1,0:T(8,128)(2,1)S(1)} %get-tuple-element.23.qt_ref, f32[4,128,512]{2,1,0:T(8,128)S(1)} %get-tuple-element.36.acc_in, ...), custom_call_target="tpu_custom_call", output_to_operand_aliasing={{0}: (2, {}), {1}: (3, {})} | custom-call | flops 1024 | bytes 1024 | tf_op jit(solution)/shard_map/pallas_call | solution.py:167
  27.1 0.0 collective-permute-done.4.refs_0_
  27.1 3.4 %collective-permute-done.5.refs_1_ = bf16[1024,128]{1,0:T(8,128)(2,1)S(1)} collective-permute-done((bf16[1024,128]{1,0:T(8,128)(2,1)S(1)}, bf16[1024,128]{1,0:T(8,128)(2,1)S(1)}, u32[]{:S(2)}, u32[]{:S(2)}) %collective-permute-start.5) | collective-permute-done | bytes 262176 | tf_op jit(solution)/shard_map/ppermute | solution.py:185
  30.5 3.8 %shard_map.62 = (f32[4,128,512]{2,1,0:T(8,128)S(1)}, f32[8,512]{1,0:T(8,128)S(1)}, bf16[512,512]{1,0:T(8,128)(2,1)}, f32[4,512]{1,0:T(4,128)}) custom-call(s32[16]{0:T(128)S(1)} %copy-done.1, bf16[4,128,512]{2,1,0:T(8,128)(2,1)S(1)} %get-tuple-element.23.qt_ref, ...), custom_call_target="tpu_custom_call", output_to_operand_aliasing={{0}: (2, {}), {1}: (3, {})} | custom-call | flops 1024 | bytes 1024 | tf_op jit(solution)/shard_map/pallas_call | solution.py:167
  (1 shorter events, 0.0 us)
Async XLA Ops:
  0.6 1.0 %copy-start.2 = (bf16[512,128]{1,0:T(8,128)(2,1)S(1)}, bf16[512,128]{1,0:T(8,128)(2,1)}, u32[]{:S(2)}) copy-start(bf16[512,128]{1,0:T(8,128)(2,1)} %param.7) | copy-start | bytes 393220
  1.6 3.5 %copy-start.1 = (s32[16]{0:T(128)S(1)}, s32[16]{0:T(128)}, u32[]{:S(2)}) copy-start(s32[16]{0:T(128)} %lengths_ref.7) | copy-start | bytes 196
  1.6 10.3 %collective-permute-start = (bf16[1024,128]{1,0:T(8,128)(2,1)S(1)}, bf16[1024,128]{1,0:T(8,128)(2,1)S(1)}, u32[]{:S(2)}, u32[]{:S(2)}) collective-permute-start(bf16[1024,128]{1,0:T(8,128)(2,1)S(1)} %constant_dynamic-update-slice_fusion.kv_ref), channel_id=1, source_target_pairs={{0,2},{1,3},{2,4},{3,5},{4,6},{5,7},{8,10},{9,11},{10,12},{11,13},... | collective-permute-start | bytes 786440 | tf_op jit(solution)/shard_map/ppermute | solution.py:185
  5.1 1.0 %copy-start = (bf16[512,512]{1,0:T(8,128)(2,1)S(1)}, bf16[512,512]{1,0:T(8,128)(2,1)}, u32[]{:S(2)}) copy-start(bf16[512,512]{1,0:T(8,128)(2,1)} %q_ref.1) | copy-start | bytes 1572868
  8.5 10.0 %collective-permute-start.2 = (bf16[1024,128]{1,0:T(8,128)(2,1)S(1)}, bf16[1024,128]{1,0:T(8,128)(2,1)S(1)}, u32[]{:S(2)}, u32[]{:S(2)}) collective-permute-start(bf16[1024,128]{1,0:T(8,128)(2,1)S(1)} %constant_dynamic-update-slice_fusion.kv_ref), channel_id=1, source_target_pairs={{0,1},{2,3},{4,5},{6,7},{1,0},{8,9},{10,11},{12,13},{14,15},{9,8},... | collective-permute-start | bytes 786440 | tf_op jit(solution)/shard_map/ppermute | solution.py:185
  12.0 9.5 %collective-permute-start.1 = (bf16[1024,128]{1,0:T(8,128)(2,1)S(1)}, bf16[1024,128]{1,0:T(8,128)(2,1)S(1)}, u32[]{:S(2)}, u32[]{:S(2)}) collective-permute-start(bf16[1024,128]{1,0:T(8,128)(2,1)S(1)} %collective-permute-done.refs_0_), channel_id=1, source_target_pairs={{2,4},{3,5},{4,6},{5,7},{10,12},{11,13},{12,14},{13,15},{18,20},{1... | collective-permute-start | bytes 786440 | tf_op jit(solution)/shard_map/ppermute | solution.py:185
  15.1 9.6 %collective-permute-start.3 = (bf16[1024,128]{1,0:T(8,128)(2,1)S(1)}, bf16[1024,128]{1,0:T(8,128)(2,1)S(1)}, u32[]{:S(2)}, u32[]{:S(2)}) collective-permute-start(bf16[1024,128]{1,0:T(8,128)(2,1)S(1)} %collective-permute-done.refs_0_), channel_id=1, source_target_pairs={{3,2},{5,4},{7,6},{2,3},{4,5},{6,7},{11,10},{13,12},{15,14},{10,11... | collective-permute-start | bytes 786440 | tf_op jit(solution)/shard_map/ppermute | solution.py:185
  20.8 6.3 %collective-permute-start.4 = (bf16[1024,128]{1,0:T(8,128)(2,1)S(1)}, bf16[1024,128]{1,0:T(8,128)(2,1)S(1)}, u32[]{:S(2)}, u32[]{:S(2)}) collective-permute-start(bf16[1024,128]{1,0:T(8,128)(2,1)S(1)} %collective-permute-done.2.refs_1_), channel_id=1, source_target_pairs={{0,6},{8,14},{16,22},{24,30}} | collective-permute-start | bytes 786440 | tf_op jit(solution)/shard_map/ppermute | solution.py:185
  21.5 9.0 %collective-permute-start.5 = (bf16[1024,128]{1,0:T(8,128)(2,1)S(1)}, bf16[1024,128]{1,0:T(8,128)(2,1)S(1)}, u32[]{:S(2)}, u32[]{:S(2)}) collective-permute-start(bf16[1024,128]{1,0:T(8,128)(2,1)S(1)} %collective-permute-done.1.refs_0_), channel_id=1, source_target_pairs={{5,4},{7,6},{4,5},{6,7},{13,12},{15,14},{12,13},{14,15},{21,20},{2... | collective-permute-start | bytes 786440 | tf_op jit(solution)/shard_map/ppermute | solution.py:185
where the time goes:
time: 34.3 us
  starting transfers between devices  17.2 us (50%)
  Pallas kernels  10.9 us (32%)
  waiting for transfers between devices  3.39 us (10%)
  local copies, waits for them, and re-layouts  2.02 us (6%)
  between operations  0.79 us (2%)
    ppermute x6, starting transfers between devices, send(): return lax.ppermute(value, 'ctx', pairs)  17.2 us
    pallas_call x3, Pallas kernels, past_part(): pl.pallas_call(functools.partial(past_kernel, distances, is_last), out_sh...  8.53 us
    ppermute x6, waiting for transfers between devices, send(): return lax.ppermute(value, 'ctx', pairs)  3.39 us
    pallas_call x1, Pallas kernels, own_part(): pl.pallas_call(own_kernel, out_shape=(jax.ShapeDtypeStruct((QH, HD, q_row...  2.34 us
    unnamed x7, local copies, waits for them, and re-layouts  2 us
  transfers between devices with their start and end apart: 6, of which 1 were waited for; matrix products, arithmetic and copies ran while one was open for 0% of the time, Pallas kernels for 21%

commit v1 on v0

--- a/solution.py
+++ b/solution.py
@@ -13,6 +13,7 @@
 LOW = -1e30
 SCALE = 1.0 / math.sqrt(HD)
 EXP2_SCALE = SCALE * math.log2(math.e)
+MOST_TOTAL = 2.0**64
 VMEM_LIMIT = 32 * 1024 * 1024
 LITTLE = pl.CostEstimate(flops=1024, bytes_accessed=1024, transcendentals=0)
 
@@ -108,6 +109,27 @@
 
         lax.fori_loop(0, jnp.where(live_rows > half, 2, 1), absorb_tile, 0)
 
+    def absorb_whole(kv_ref):
+        scores = dot(kv_ref[:q_rows], side_by_side(lambda h: qt_ref[h]))
+        top = side_by_side(lambda h: stat_ref[h : h + 1, :])
+        weights = jnp.exp2((scores - top) * EXP2_SCALE)
+        total = jnp.sum(weights, axis=0, keepdims=True)
+        mixed = dot(jnp.transpose(kv_ref[q_rows:]), weights.astype(jnp.bfloat16))
+        live = lax.broadcasted_iota(jnp.int32, (1, q_rows), 1) < live_rows
+        live = side_by_side(lambda h: live)
+        total = jnp.where(live, total, 0.0)
+        fits = jnp.max(total) < MOST_TOTAL
+
+        @pl.when(fits)
+        def _():
+            added = jnp.where(live, mixed, 0.0)
+            for h in range(QH):
+                part = slice(h * q_rows, (h + 1) * q_rows)
+                acc_ref[h] += added[:, part]
+                stat_ref[QH + h : QH + h + 1, :] += total[:, part]
+
+        return fits
+
     last_pair = here >= lax.axis_size("ctx") - 2
     for kv_ref, (even_distance, odd_distance, only) in zip(kv_refs, distances):
         distance = jnp.where(odd == 1, odd_distance, even_distance)
@@ -115,9 +137,11 @@
         seen = (distance > 0) & (live_rows > 0) & (cut < q_rows)
         if only is not None:
             seen = seen & (last_pair == only)
-        wide = (cut <= 0) & (live_rows > half)
-        pl.when(seen & wide)(functools.partial(absorb, kv_ref, q_rows, slice(0, q_rows)))
-        pl.when(seen & jnp.logical_not(wide) & (cut < half))(
+        wide = seen & (cut <= 0) & (live_rows > half)
+        added = lax.cond(
+            wide, functools.partial(absorb_whole, kv_ref), lambda: jnp.bool_(False)
+        )
+        pl.when(seen & jnp.logical_not(added) & (cut < half))(
             functools.partial(absorb_tiles, kv_ref, 0, cut)
         )
         pl.when(seen & (cut >= half))(functools.partial(absorb_tiles, kv_ref, half, cut))

time: 34.3 us -> 33.4 us (0.974)
  Pallas kernels: 10.9 us -> 10 us
  waiting for transfers between devices: 3.39 us -> 3.85 us
    pallas_call x3, Pallas kernels: 8.53 us -> 7.7 us  [past_part(): pl.pallas_call(functools.partial(past_kernel, distances, is_last), out_sh...]
    ppermute x6, waiting for transfers between devices: 3.39 us -> 3.85 us  [send(): return lax.ppermute(value, 'ctx', pairs)]
  transfers between devices with their start and end apart: 6 -> 6, of which waited for: 1 -> 2; matrix products, arithmetic and copies ran while one was open for 0% -> 0% of each run, Pallas kernels for 21% -> 19%
where the time goes in v1:
time: 33.4 us; the launch traced here: 33.6 us
  starting transfers between devices  16.9 us (51%)
  Pallas kernels  10 us (30%)
  waiting for transfers between devices  3.85 us (12%)
  local copies, waits for them, and re-layouts  2.02 us (6%)
  between operations  0.78 us (2%)
    ppermute x6, starting transfers between devices, send(): return lax.ppermute(value, 'ctx', pairs)  16.9 us
    pallas_call x3, Pallas kernels, past_part(): pl.pallas_call(functools.partial(past_kernel, distances, is_last), out_sh...  7.7 us
    ppermute x6, waiting for transfers between devices, send(): return lax.ppermute(value, 'ctx', pairs)  3.85 us
    pallas_call x1, Pallas kernels, own_part(): pl.pallas_call(own_kernel, out_shape=(jax.ShapeDtypeStruct((QH, HD, q_row...  2.34 us
    unnamed x7, local copies, waits for them, and re-layouts  2 us
  transfers between devices with their start and end apart: 6, of which 2 were waited for; matrix products, arithmetic and copies ran while one was open for 0% of the time, Pallas kernels for 19%

profile of v1, /device:TPU:16, one launch (start us, length us, event | category | flops | bytes accessed | tf_op | source)
XLA Modules:
  0.0 33.6 jit_solution(11403002168081457857)
XLA Ops:
  0.6 0.0 copy-start.2
  0.6 0.9 %constant_dynamic-update-slice_fusion.1 = bf16[1024,128]{1,0:T(8,128)(2,1)S(1)} fusion(bf16[512,128]{1,0:T(8,128)(2,1)} %param.6), kind=kLoop, calls=%fused_computation.1 | loop fusion | bytes 262144
  1.6 0.0 copy-done.2
  1.6 0.0 copy-start.1
  1.6 3.5 %collective-permute-start = (bf16[1024,128]{1,0:T(8,128)(2,1)S(1)}, bf16[1024,128]{1,0:T(8,128)(2,1)S(1)}, u32[]{:S(2)}, u32[]{:S(2)}) collective-permute-start(bf16[1024,128]{1,0:T(8,128)(2,1)S(1)} %constant_dynamic-update-slice_fusion.kv_ref), channel_id=1, source_target_pairs={{0,2},{1,3},{2,4},{3,5},{4,6},{5,7},{8,10},{9,11},{10,12},{11,13},... | collective-permute-start | bytes 786440 | tf_op jit(solution)/shard_map/ppermute | solution.py:209
  5.1 0.0 copy-done.1
  5.1 0.0 copy-start
  5.2 1.0 %copy-done = bf16[512,512]{1,0:T(8,128)(2,1)S(1)} copy-done((bf16[512,512]{1,0:T(8,128)(2,1)S(1)}, bf16[512,512]{1,0:T(8,128)(2,1)}, u32[]{:S(2)}) %copy-start) | copy-done | bytes 524312
  6.2 2.3 %shard_map.59 = (bf16[4,128,512]{2,1,0:T(8,128)(2,1)S(1)}, f32[4,128,512]{2,1,0:T(8,128)S(1)}, f32[8,512]{1,0:T(8,128)S(1)}) custom-call(s32[16]{0:T(128)S(1)} %copy-done.1, bf16[512,512]{1,0:T(8,128)(2,1)S(1)} %copy-done, bf16[1024,128]{1,0:T(8,128)(2,1)S(1)} %constant_dynamic-update-slice_fusion.kv_ref), custom_call_target="tpu_custom_call" | custom-call | flops 1024 | bytes 1024 | tf_op jit(solution)/shard_map/pallas_call | solution.py:168
  8.5 3.4 %collective-permute-start.2 = (bf16[1024,128]{1,0:T(8,128)(2,1)S(1)}, bf16[1024,128]{1,0:T(8,128)(2,1)S(1)}, u32[]{:S(2)}, u32[]{:S(2)}) collective-permute-start(bf16[1024,128]{1,0:T(8,128)(2,1)S(1)} %constant_dynamic-update-slice_fusion.kv_ref), channel_id=1, source_target_pairs={{0,1},{2,3},{4,5},{6,7},{1,0},{8,9},{10,11},{12,13},{14,15},{9,8},... | collective-permute-start | bytes 786440 | tf_op jit(solution)/shard_map/ppermute | solution.py:209
  12.0 0.0 collective-permute-done.refs_0_
  12.0 3.1 %collective-permute-start.1 = (bf16[1024,128]{1,0:T(8,128)(2,1)S(1)}, bf16[1024,128]{1,0:T(8,128)(2,1)S(1)}, u32[]{:S(2)}, u32[]{:S(2)}) collective-permute-start(bf16[1024,128]{1,0:T(8,128)(2,1)S(1)} %collective-permute-done.refs_0_), channel_id=1, source_target_pairs={{2,4},{3,5},{4,6},{5,7},{10,12},{11,13},{12,14},{13,15},{18,20},{1... | collective-permute-start | bytes 786440 | tf_op jit(solution)/shard_map/ppermute | solution.py:209
  15.1 3.4 %collective-permute-start.3 = (bf16[1024,128]{1,0:T(8,128)(2,1)S(1)}, bf16[1024,128]{1,0:T(8,128)(2,1)S(1)}, u32[]{:S(2)}, u32[]{:S(2)}) collective-permute-start(bf16[1024,128]{1,0:T(8,128)(2,1)S(1)} %collective-permute-done.refs_0_), channel_id=1, source_target_pairs={{3,2},{5,4},{7,6},{2,3},{4,5},{6,7},{11,10},{13,12},{15,14},{10,11... | collective-permute-start | bytes 786440 | tf_op jit(solution)/shard_map/ppermute | solution.py:209
  18.5 0.0 collective-permute-done.2.refs_1_
  18.5 1.9 %shard_map.60 = (f32[4,128,512]{2,1,0:T(8,128)S(1)}, f32[8,512]{1,0:T(8,128)S(1)}) custom-call(s32[16]{0:T(128)S(1)} %copy-done.1, bf16[4,128,512]{2,1,0:T(8,128)(2,1)S(1)} %get-tuple-element.23.qt_ref, f32[4,128,512]{2,1,0:T(8,128)S(1)} %get-tuple-element.30.acc_in, ...), custom_call_target="tpu_custom_call", output_to_operand_aliasing={{0}: (2, {}), {1}: (3, {})} | custom-call | flops 1024 | bytes 1024 | tf_op jit(solution)/shard_map/pallas_call | solution.py:191
  20.4 0.7 %collective-permute-start.4 = (bf16[1024,128]{1,0:T(8,128)(2,1)S(1)}, bf16[1024,128]{1,0:T(8,128)(2,1)S(1)}, u32[]{:S(2)}, u32[]{:S(2)}) collective-permute-start(bf16[1024,128]{1,0:T(8,128)(2,1)S(1)} %collective-permute-done.2.refs_1_), channel_id=1, source_target_pairs={{0,6},{8,14},{16,22},{24,30}} | collective-permute-start | bytes 786440 | tf_op jit(solution)/shard_map/ppermute | solution.py:209
  21.1 0.3 collective-permute-done.1.refs_0_
  21.4 2.8 %collective-permute-start.5 = (bf16[1024,128]{1,0:T(8,128)(2,1)S(1)}, bf16[1024,128]{1,0:T(8,128)(2,1)S(1)}, u32[]{:S(2)}, u32[]{:S(2)}) collective-permute-start(bf16[1024,128]{1,0:T(8,128)(2,1)S(1)} %collective-permute-done.1.refs_0_), channel_id=1, source_target_pairs={{5,4},{7,6},{4,5},{6,7},{13,12},{15,14},{12,13},{14,15},{21,20},{2... | collective-permute-start | bytes 786440 | tf_op jit(solution)/shard_map/ppermute | solution.py:209
  24.2 0.0 collective-permute-done.3.refs_2_
  24.2 2.1 %shard_map.61 = (f32[4,128,512]{2,1,0:T(8,128)S(1)}, f32[8,512]{1,0:T(8,128)S(1)}) custom-call(s32[16]{0:T(128)S(1)} %copy-done.1, bf16[4,128,512]{2,1,0:T(8,128)(2,1)S(1)} %get-tuple-element.23.qt_ref, f32[4,128,512]{2,1,0:T(8,128)S(1)} %get-tuple-element.36.acc_in, ...), custom_call_target="tpu_custom_call", output_to_operand_aliasing={{0}: (2, {}), {1}: (3, {})} | custom-call | flops 1024 | bytes 1024 | tf_op jit(solution)/shard_map/pallas_call | solution.py:191
  26.3 0.0 collective-permute-done.4.refs_0_
  26.3 3.5 %collective-permute-done.5.refs_1_ = bf16[1024,128]{1,0:T(8,128)(2,1)S(1)} collective-permute-done((bf16[1024,128]{1,0:T(8,128)(2,1)S(1)}, bf16[1024,128]{1,0:T(8,128)(2,1)S(1)}, u32[]{:S(2)}, u32[]{:S(2)}) %collective-permute-start.5) | collective-permute-done | bytes 262176 | tf_op jit(solution)/shard_map/ppermute | solution.py:209
  29.8 3.8 %shard_map.62 = (f32[4,128,512]{2,1,0:T(8,128)S(1)}, f32[8,512]{1,0:T(8,128)S(1)}, bf16[512,512]{1,0:T(8,128)(2,1)}, f32[4,512]{1,0:T(4,128)}) custom-call(s32[16]{0:T(128)S(1)} %copy-done.1, bf16[4,128,512]{2,1,0:T(8,128)(2,1)S(1)} %get-tuple-element.23.qt_ref, ...), custom_call_target="tpu_custom_call", output_to_operand_aliasing={{0}: (2, {}), {1}: (3, {})} | custom-call | flops 1024 | bytes 1024 | tf_op jit(solution)/shard_map/pallas_call | solution.py:191
  (1 shorter events, 0.0 us)
Async XLA Ops:
  0.6 1.0 %copy-start.2 = (bf16[512,128]{1,0:T(8,128)(2,1)S(1)}, bf16[512,128]{1,0:T(8,128)(2,1)}, u32[]{:S(2)}) copy-start(bf16[512,128]{1,0:T(8,128)(2,1)} %param.7) | copy-start | bytes 393220
  1.6 3.5 %copy-start.1 = (s32[16]{0:T(128)S(1)}, s32[16]{0:T(128)}, u32[]{:S(2)}) copy-start(s32[16]{0:T(128)} %lengths_ref.7) | copy-start | bytes 196
  1.6 10.3 %collective-permute-start = (bf16[1024,128]{1,0:T(8,128)(2,1)S(1)}, bf16[1024,128]{1,0:T(8,128)(2,1)S(1)}, u32[]{:S(2)}, u32[]{:S(2)}) collective-permute-start(bf16[1024,128]{1,0:T(8,128)(2,1)S(1)} %constant_dynamic-update-slice_fusion.kv_ref), channel_id=1, source_target_pairs={{0,2},{1,3},{2,4},{3,5},{4,6},{5,7},{8,10},{9,11},{10,12},{11,13},... | collective-permute-start | bytes 786440 | tf_op jit(solution)/shard_map/ppermute | solution.py:209
  5.1 1.0 %copy-start = (bf16[512,512]{1,0:T(8,128)(2,1)S(1)}, bf16[512,512]{1,0:T(8,128)(2,1)}, u32[]{:S(2)}) copy-start(bf16[512,512]{1,0:T(8,128)(2,1)} %q_ref.1) | copy-start | bytes 1572868
  8.5 10.0 %collective-permute-start.2 = (bf16[1024,128]{1,0:T(8,128)(2,1)S(1)}, bf16[1024,128]{1,0:T(8,128)(2,1)S(1)}, u32[]{:S(2)}, u32[]{:S(2)}) collective-permute-start(bf16[1024,128]{1,0:T(8,128)(2,1)S(1)} %constant_dynamic-update-slice_fusion.kv_ref), channel_id=1, source_target_pairs={{0,1},{2,3},{4,5},{6,7},{1,0},{8,9},{10,11},{12,13},{14,15},{9,8},... | collective-permute-start | bytes 786440 | tf_op jit(solution)/shard_map/ppermute | solution.py:209
  12.0 9.4 %collective-permute-start.1 = (bf16[1024,128]{1,0:T(8,128)(2,1)S(1)}, bf16[1024,128]{1,0:T(8,128)(2,1)S(1)}, u32[]{:S(2)}, u32[]{:S(2)}) collective-permute-start(bf16[1024,128]{1,0:T(8,128)(2,1)S(1)} %collective-permute-done.refs_0_), channel_id=1, source_target_pairs={{2,4},{3,5},{4,6},{5,7},{10,12},{11,13},{12,14},{13,15},{18,20},{1... | collective-permute-start | bytes 786440 | tf_op jit(solution)/shard_map/ppermute | solution.py:209
  15.1 9.1 %collective-permute-start.3 = (bf16[1024,128]{1,0:T(8,128)(2,1)S(1)}, bf16[1024,128]{1,0:T(8,128)(2,1)S(1)}, u32[]{:S(2)}, u32[]{:S(2)}) collective-permute-start(bf16[1024,128]{1,0:T(8,128)(2,1)S(1)} %collective-permute-done.refs_0_), channel_id=1, source_target_pairs={{3,2},{5,4},{7,6},{2,3},{4,5},{6,7},{11,10},{13,12},{15,14},{10,11... | collective-permute-start | bytes 786440 | tf_op jit(solution)/shard_map/ppermute | solution.py:209
  20.4 5.9 %collective-permute-start.4 = (bf16[1024,128]{1,0:T(8,128)(2,1)S(1)}, bf16[1024,128]{1,0:T(8,128)(2,1)S(1)}, u32[]{:S(2)}, u32[]{:S(2)}) collective-permute-start(bf16[1024,128]{1,0:T(8,128)(2,1)S(1)} %collective-permute-done.2.refs_1_), channel_id=1, source_target_pairs={{0,6},{8,14},{16,22},{24,30}} | collective-permute-start | bytes 786440 | tf_op jit(solution)/shard_map/ppermute | solution.py:209
  21.4 8.4 %collective-permute-start.5 = (bf16[1024,128]{1,0:T(8,128)(2,1)S(1)}, bf16[1024,128]{1,0:T(8,128)(2,1)S(1)}, u32[]{:S(2)}, u32[]{:S(2)}) collective-permute-start(bf16[1024,128]{1,0:T(8,128)(2,1)S(1)} %collective-permute-done.1.refs_0_), channel_id=1, source_target_pairs={{5,4},{7,6},{4,5},{6,7},{13,12},{15,14},{12,13},{14,15},{21,20},{2... | collective-permute-start | bytes 786440 | tf_op jit(solution)/shard_map/ppermute | solution.py:209
